TPU v7x, 128 devices: a whole 4x4x4 slice. The times are simulated.
128 devices in a mesh: mp: 4 (over x_hi, core), lat: 32 (over y, z, x_lo).
Axes of the slice: x: 4 (x_hi: 2, x_lo: 2; x = x_hi * 2 + x_lo), y: 4, z: 4, core: 2. Of those that a mesh axis runs over, the one named last changes fastest.
Arguments:
- resid_in: bfloat16 [1024, 2304], P('lat'), may hold values from -6 to 6
- layer_terms: bfloat16 [4, 1024, 2304], P('mp', 'lat'), may hold values from -4 to 4
- dec_bias: float32 [2304], replicated, may hold values from -3 to 3
- enc_weight: bfloat16 [2304, 65536], P(None, ('mp', 'lat')), may hold values from -0.125 to 0.125
- enc_bias: float32 [65536], P(('mp', 'lat')), may hold values from -4.5 to -2
- dec_weight: bfloat16 [65536, 2304], P(('mp', 'lat')), may hold values from -0.25 to 0.25
- first_moment: float32 [2304, 65536], P(None, ('mp', 'lat')), may hold values from -0.6 to 0.6
- second_moment: float32 [2304, 65536], P(None, ('mp', 'lat')), may hold values from 0.002 to 0.3
Outputs:
- enc_weight_new: bfloat16 [2304, 65536], P(None, ('mp', 'lat'))
- first_moment_new: float32 [2304, 65536], P(None, ('mp', 'lat'))
- second_moment_new: float32 [2304, 65536], P(None, ('mp', 'lat'))
- recon_error: bfloat16 [1024, 2304], P(('mp', 'lat'))
All inputs are finite; a program needn't handle non-finite values.
Results may differ from a plain program's by a relative error of at most 0.02.
The roundings to bfloat16 on the way count: a program that leaves them out, or rounds other values in their place, can miss the bound.
Values may be sent and summed in bfloat16 or wider, within the bound.
A program may use at most 128 MiB of HBM per device.

v0:
```python
import jax
import jax.numpy as jnp
from jax import lax
from jax.sharding import PartitionSpec as P

ROWS_DEV = 8
STEP = 10


l1_coeff = 5.0
loss_norm = 32.0
beta_one = 0.9
beta_two = 0.95
learn_rate = 0.001
adam_eps = 1e-08


def on_device(
    resid_in, layer_terms, dec_bias, enc_weight, enc_bias, dec_weight, first_moment, second_moment
):
    lat_count = lax.axis_size("lat")
    mp_count = lax.axis_size("mp")
    width = resid_in.shape[1]
    term = layer_terms[0].astype(jnp.float32)
    share = lax.psum_scatter(term, "mp", scatter_dimension=1, tiled=True)
    feat = width // mp_count
    offset = lax.axis_index("mp") * feat
    own_in = lax.dynamic_slice_in_dim(resid_in, offset, feat, 1)
    own_bias = lax.dynamic_slice_in_dim(dec_bias, offset, feat, 0)
    share_rows = (own_in.astype(jnp.float32) + share - own_bias).astype(jnp.bfloat16)
    centered_rows = lax.all_gather(share_rows, "mp", axis=1, tiled=True)
    piece = lax.all_gather(centered_rows, "lat", axis=0, tiled=True)
    pre = jnp.dot(piece, enc_weight, preferred_element_type=jnp.float32) + enc_bias
    active = jnp.maximum(pre, 0.0).astype(jnp.bfloat16)
    norms = jnp.sqrt(jnp.sum(jnp.square(dec_weight.astype(jnp.float32)), axis=1))
    block = lax.axis_index("mp") * lat_count + lax.axis_index("lat")
    own_centered = lax.dynamic_slice_in_dim(piece, block * ROWS_DEV, ROWS_DEV, 0)
    recon = lax.psum_scatter(
        jnp.dot(active, dec_weight, preferred_element_type=jnp.float32),
        ("mp", "lat"),
        scatter_dimension=0,
        tiled=True,
    )
    recon_error = (recon - own_centered.astype(jnp.float32)).astype(jnp.bfloat16)
    back = lax.dot_general(
        lax.all_gather(recon_error, ("mp", "lat"), axis=0, tiled=True),
        dec_weight,
        (((1,), (1,)), ((), ())),
        preferred_element_type=jnp.float32,
    )
    live = active > 0
    slopes = jnp.where(live, back * (2.0 / loss_norm) + l1_coeff / loss_norm * norms, 0.0).astype(
        jnp.bfloat16
    )
    grad = lax.dot_general(
        piece, slopes, (((0,), (0,)), ((), ())), preferred_element_type=jnp.float32
    )
    corr_one = 1.0 - beta_one**STEP
    corr_two = 1.0 - beta_two**STEP
    first_new = beta_one * first_moment + (1.0 - beta_one) * grad
    second_new = beta_two * second_moment + (1.0 - beta_two) * grad * grad
    change = first_new / corr_one / (jnp.sqrt(second_new / corr_two) + adam_eps)
    weight_new = (enc_weight.astype(jnp.float32) - learn_rate * change).astype(jnp.bfloat16)
    return (weight_new, first_new, second_new, recon_error)


def solution(mesh):
    in_specs = (
        P("lat", None),
        P("mp", "lat", None),
        P(),
        P(None, ("mp", "lat")),
        P(("mp", "lat")),
        P(("mp", "lat"), None),
        P(None, ("mp", "lat")),
        P(None, ("mp", "lat")),
    )
    out_specs = (
        P(None, ("mp", "lat")),
        P(None, ("mp", "lat")),
        P(None, ("mp", "lat")),
        P(("mp", "lat"), None),
    )
    return jax.shard_map(
        on_device, mesh=mesh, in_specs=in_specs, out_specs=out_specs, check_vma=False
    )
```

profile of v0, /device:TPU:1, one launch (start us, length us, event | category | flops | bytes accessed | tf_op | source)
XLA Modules:
  0.0 1223.2 jit_solution(17312635340249548544)
XLA Ops:
  7.2 0.0 reduce-scatter.7.cloned.1.call-start
  7.2 0.9 bitcast_convert_fusion
  8.1 1.4 copy.14
  9.5 0.0 reduce-scatter.7.cloned.1.call-update
  9.6 0.0 all-gather.4.cloned.1.call-start
  9.6 0.8 dynamic_slice.10
  10.4 36.7 %reduce-scatter.7.cloned.1.call-done = f32[576,32]{1,0:T(8,128)} async-done(((f32[2304,32]{1,0:T(8,128)}), f32[576,32]{1,0:T(8,128)}) %reduce-scatter.7.cloned.1.call-update) | async-done | bytes 73744
  47.1 1.1 copy.15
  48.2 0.9 fusion.2
  49.1 7.5 all-gather
  56.6 0.1 copy.13
  56.7 0.8 reshape.18
  57.5 0.0 all-gather.4.cloned.1.call-update
  57.5 0.0 copy-start
  57.6 0.0 reduce-scatter.5.cloned.1.call-start
  57.6 146.9 %all-gather.4.cloned.1.call-done = bf16[1024,2304]{1,0:T(8,128)(2,1)} async-done(((bf16[32,2304]{1,0:T(8,128)(2,1)}), bf16[1024,2304]{1,0:T(8,128)(2,1)}) %all-gather.4.cloned.1.call-update) | async-done | bytes 4718608 | tf_op jit(solution)/shard_map/all_gather | solution.py:32
  204.5 5.6 maximum_convert_fusion
  210.1 0.0 copy-done
  210.1 5.0 fusion.7
  215.2 0.0 reduce-scatter.5.cloned.1.call-update
  215.2 0.0 all-gather.6.cloned.1.call-start
  215.2 614.7 %reduce-scatter.5.cloned.1.call-done = f32[8,2304]{1,0:T(8,128)} async-done(((f32[1024,2304]{1,0:T(8,128)}), f32[8,2304]{1,0:T(8,128)}) %reduce-scatter.5.cloned.1.call-update) | async-done | bytes 73744 | tf_op jit(solution)/shard_map/reduce_scatter | solution.py:38
  830.0 1.5 subtract_convert_fusion.2
  831.5 0.0 all-gather.6.cloned.1.call-update
  831.5 0.5 multiply_reduce_fusion
  832.0 363.6 %all-gather.6.cloned.1.call-done = bf16[1024,2304]{1,0:T(8,128)(2,1)} async-done(((bf16[8,2304]{1,0:T(8,128)(2,1)}), bf16[1024,2304]{1,0:T(8,128)(2,1)}) %all-gather.6.cloned.1.call-update) | async-done | bytes 4718608 | tf_op jit(solution)/shard_map/all_gather | solution.py:46
  1195.6 21.0 %subtract_convert_fusion = (bf16[2304,512]{1,0:T(8,128)(2,1)}, f32[2304,512]{1,0:T(8,128)}, f32[2304,512]{1,0:T(8,128)}) fusion(bf16[2304,512]{1,0:T(8,128)(2,1)} %param.11, f32[2304,512]{1,0:T(8,128)} %param.14, f32[2304,512]{1,0:T(8,128)} %param.15, bf16[1024,2304]{1,0:T(8,128)(2,1)} %all-gather.4.cloned.1.call-done, ...), kind=kOutput, calls=%fused_computation.2 | convolution fusion | flops 4852154368 | bytes 36440064 | tf_op jit(solution)/shard_map/dot_general | solution.py:55
  (1 shorter events, 0.0 us)
Async XLA Ops:
  7.2 39.9 %reduce-scatter.7.cloned.1.call-start = ((), (), s32[]{:S(2)}) async-start(), calls=%async_computation.5 | async-start | bytes 1474560
  9.6 194.9 %all-gather.4.cloned.1.call-start = ((), (), s32[]{:S(2)}) async-start(), calls=%async_computation.2 | async-start | bytes 4866048 | tf_op jit(solution)/shard_map/all_gather | solution.py:32
  57.5 152.6 %copy-start = (bf16[512,2304]{1,0:T(8,128)(2,1)S(1)}, bf16[512,2304]{1,0:T(8,128)(2,1)}, u32[]{:S(2)}) copy-start(bf16[512,2304]{1,0:T(8,128)(2,1)} %param.13) | copy-start | bytes 7077892
  57.6 772.4 %reduce-scatter.5.cloned.1.call-start = ((), (), s32[]{:S(2)}) async-start(), calls=%async_computation.3 | async-start | bytes 9510912 | tf_op jit(solution)/shard_map/reduce_scatter | solution.py:38
  215.2 980.4 %all-gather.6.cloned.1.call-start = ((), (), s32[]{:S(2)}) async-start(), calls=%async_computation.4 | async-start | bytes 4755456 | tf_op jit(solution)/shard_map/all_gather | solution.py:46
Sparse Core Ops, SparseCore 0:
  11.2 35.8 reduce-scatter.6
  57.7 146.7 all-gather.3
  215.3 614.6 reduce-scatter.4
  832.2 363.3 all-gather.5
where the time goes:
time: 1220 us
  waiting for transfers between devices  1160 us (95%)
  matrix products  31.7 us (3%)
  between operations  13.8 us (1%)
    reduce_scatter x1, waiting for transfers between devices, on_device(): lax.psum_scatter(jnp.dot(active, dec_weight, preferred_element_type=jnp.f...  615 us
    all_gather x1, waiting for transfers between devices, on_device(): lax.all_gather(recon_error, ('mp', 'lat'), axis=0, tiled=True)  364 us
    all_gather x1, waiting for transfers between devices, on_device(): piece = lax.all_gather(centered_rows, 'lat', axis=0, tiled=True)  147 us
    unnamed x5, waiting for transfers between devices  36.8 us
  transfers between devices with their start and end apart: 4, of which 4 were waited for; matrix products, arithmetic and copies ran while one was open for 0% of the time, Pallas kernels for 0%

commit v1 on v0

v1 whole, which is shorter than its diff:
```python
import jax
import jax.numpy as jnp
from jax import lax
from jax.experimental import pallas as pl
from jax.experimental.pallas import tpu as pltpu
from jax.sharding import PartitionSpec as P

MESH = pl.DeviceIdType.MESH
STEP = 10
l1_coeff = 5.0
loss_norm = 32.0
beta_one = 0.9
beta_two = 0.95
learn_rate = 0.001
adam_eps = 1e-08

D = 2304
HALF = D // 2
GROUP = HALF // 3
PARTS = 3
LAT_DEV = 512
ROWS = 1024
BLOCK = 16
TILE = 256
ORDER = ((2, 1, 0), (0, 2, 1), (1, 0, 2))


def exchange_kernel(
    resid, terms, dec_bias, enc_weight, enc_bias, dec_weight,
    slopes_out, centered_t_out, error_out,
    cen, err, cen_t, weight, dec, dec_t, norms, codes, cross_send, cross_recv, part_sum,
    a_send, a_recv, b_send, b_recv, c_send, c_recv, d_send, d_recv, sum_two, slopes,
    term_in, resid_in, bias_in, enc_bias_in, own_cen,
    send_sems, recv_sems, local_sems,
):
    m = lax.axis_index("mp")
    lat = lax.axis_index("lat")
    core = lax.rem(m, 2)
    yz = lax.div(lat, 2)
    x = lax.div(m, 2) * 2 + lax.rem(lat, 2)
    pos = (x, lax.div(yz, 4), lax.rem(yz, 4))

    def device(at, on_core):
        return (lax.div(at[0], 2) * 2 + on_core, (at[1] * 4 + at[2]) * 2 + lax.rem(at[0], 2))

    def along(axis, k):
        return lax.rem(pos[axis] + k, 4)

    def peer(axis, k):
        at = list(pos)
        at[axis] = along(axis, k)
        return device(at, core)

    other = device(pos, 1 - core)
    g0 = core * PARTS

    count = [0, 0]
    sent = []

    def remote(src, dst, to):
        i = count[0]
        count[0] += 1
        copy = pltpu.make_async_remote_copy(
            src_ref=src, dst_ref=dst, send_sem=send_sems.at[i], recv_sem=recv_sems.at[i],
            device_id=to, device_id_type=MESH,
        )
        copy.start()
        sent.append(copy)
        return copy

    def local(src, dst):
        i = count[1]
        count[1] += 1
        copy = pltpu.make_async_copy(src, dst, local_sems.at[i])
        copy.start()
        return copy

    rows16 = pl.ds(pl.multiple_of(lax.div(m, 2) * BLOCK, BLOCK), BLOCK)
    half = pl.ds(pl.multiple_of(core * HALF, 128), HALF)
    early = [
        local(terms.at[0, rows16, half], term_in.at[0]),
        local(resid.at[rows16, half], resid_in),
        local(dec_bias.at[:, half], bias_in),
        local(enc_bias, enc_bias_in),
    ]
    load_dec = [local(dec_weight.at[:, pl.ds(h * HALF, HALF)], dec.at[h]) for h in range(2)]
    load_weight = local(enc_weight, weight)

    barrier = pltpu.get_barrier_semaphore()
    greet = [other, device((lax.rem(x + 2, 4), pos[1], pos[2]), 1 - core)]
    greet += [peer(axis, k) for axis in range(3) for k in (1, 2, 3)]
    for to in greet:
        pl.semaphore_signal(barrier, inc=1, device_id=to, device_id_type=MESH)
    pl.semaphore_wait(barrier, len(greet))

    moves = []
    for k in (1, 2, 3):
        mt = lax.rem(m + k, 4)
        moves.append(
            remote(
                terms.at[
                    0,
                    pl.ds(pl.multiple_of(lax.div(mt, 2) * BLOCK, BLOCK), BLOCK),
                    pl.ds(pl.multiple_of(lax.rem(mt, 2) * HALF, 128), HALF),
                ],
                term_in.at[k],
                (mt, lat),
            )
        )
    for copy in early:
        copy.wait()
    for copy in moves:
        copy.wait_recv()
    total = term_in[0].astype(jnp.float32)
    for k in (1, 2, 3):
        total = total + term_in[k].astype(jnp.float32)
    own = (resid_in[...].astype(jnp.float32) + total - bias_in[...]).astype(jnp.bfloat16)
    for p in range(PARTS):
        own_cen[p] = own[:, p * GROUP : (p + 1) * GROUP]

    def place(sel):
        return (
            pl.ds(*sel[0]),
            pl.ds(*sel[1]),
            pl.ds(pl.multiple_of(sel[2][0] * BLOCK, BLOCK), sel[2][1] * BLOCK),
        )

    def only(base, axis, start, size):
        sel = list(base)
        sel[axis] = (start, size)
        return sel

    own_sel = [(pos[0], 1), (pos[1], 1), (pos[2], 1)]
    full = [(0, 4), (0, 4), (0, 4)]
    CUT = (1, 0, 0)

    def gather(buf, blocks, fill_one, fill_two, fill_three):
        def at(p, sel):
            return buf.at[(g0 + p,) + place(sel)]

        def share(p, sel, to):
            return remote(at(p, sel), at(p, sel), to)

        for p in range(PARTS):
            buf[(g0 + p,) + place(own_sel)] = blocks[p][None, None]
        one, two, three, four, across = [], [], [], [], []
        for p in range(PARTS):
            one.append([share(p, own_sel, peer(ORDER[p][0], k)) for k in (1, 3, 2)])
        fill_one()
        for p in range(PARTS):
            for copy in one[p]:
                copy.wait_recv()
            sel = only(own_sel, ORDER[p][0], 0, 4)
            two.append([share(p, sel, peer(ORDER[p][1], k)) for k in (1, 3, 2)])
        fill_two()
        for p in range(PARTS):
            for copy in two[p]:
                copy.wait_recv()
            axis = ORDER[p][2]
            sel = only(full, axis, pos[axis], 1)
            three.append([share(p, sel, peer(axis, k)) for k in (1, 3)])
            across.append(share(p, sel, other))
        fill_three()
        for p in range(PARTS):
            axis = ORDER[p][2]
            step = []
            for way, k in ((0, 1), (1, 3)):
                three[p][way].wait_recv()
                sel = only(full, axis, along(axis, 4 - k), 1)
                step.append(share(p, only(sel, CUT[p], way * 2, 2), peer(axis, k)))
                across.append(share(p, sel, other))
            four.append(step)
        for p in range(PARTS):
            axis = ORDER[p][2]
            sel = only(full, axis, along(axis, 2), 1)
            for way in range(2):
                four[p][way].wait_recv()
                across.append(share(p, only(sel, CUT[p], way * 2, 2), other))
        for copy in across:
            copy.wait_recv()

    def nothing():
        pass

    def turn_dec():
        for copy in load_dec:
            copy.wait()

        @pl.loop(0, 2)
        def _(h):
            for q in range(PARTS):
                dec_t[pl.ds(pl.multiple_of(h * HALF + q * GROUP, 128), GROUP), :] = dec[
                    h, :, q * GROUP : (q + 1) * GROUP
                ].T

        norms[...] = jnp.zeros_like(norms)

        @pl.loop(0, 9)
        def _(r):
            rows = dec_t[pl.ds(pl.multiple_of(r * 256, 256), 256), :].astype(jnp.float32)
            norms[...] += jnp.sum(rows * rows, axis=0, keepdims=True)

        norms[...] = jnp.sqrt(norms[...]) * (l1_coeff / loss_norm)

    gather(cen, [own_cen[p] for p in range(PARTS)], nothing, nothing, turn_dec)

    def wide(buf, t):
        return jnp.concatenate([buf[g, t].reshape(TILE, GROUP) for g in range(2 * PARTS)], axis=1)

    load_weight.wait()

    @pl.loop(0, ROWS // TILE)
    def _(t):
        pre = jnp.dot(wide(cen, t), weight[...], preferred_element_type=jnp.float32)
        codes[t] = jnp.maximum(pre + enc_bias_in[...], 0.0).astype(jnp.bfloat16)

    crossing = []
    for t in range(ROWS // TILE):
        made = jnp.dot(codes[t], dec[1 - core], preferred_element_type=jnp.float32)
        for p in range(PARTS):
            cross_send[p, t] = (
                made[:, p * GROUP : (p + 1) * GROUP].astype(jnp.bfloat16).reshape(4, 64, GROUP)
            )
        crossing.append(remote(cross_send.at[:, t], cross_recv.at[:, t], other))

    @pl.loop(0, ROWS // TILE)
    def _(t):
        made = jnp.dot(codes[t], dec[core], preferred_element_type=jnp.float32)
        for p in range(PARTS):
            part_sum[p, t] = made[:, p * GROUP : (p + 1) * GROUP].reshape(4, 64, GROUP)

    for copy in crossing:
        copy.wait_recv()

    def here(p, sel):
        where = (p,) + place(sel)
        value = part_sum[where] + cross_recv[where].astype(jnp.float32)
        return value.reshape(-1, GROUP)

    def turn_centered(first, last):
        @pl.loop(0, ROWS // TILE)
        def _(t):
            for g in range(first, last):
                cen_t[g * GROUP : (g + 1) * GROUP, pl.ds(pl.multiple_of(t * TILE, TILE), TILE)] = (
                    cen[g, t].reshape(TILE, GROUP).T
                )

    step_a = []
    for p in range(PARTS):
        axis = ORDER[p][2]
        far = only(full, axis, along(axis, 2), 1)
        step = []
        for way, k in ((0, 1), (1, 3)):
            a_send[p, way] = here(p, only(far, CUT[p], way * 2, 2)).astype(jnp.bfloat16)
            step.append(remote(a_send.at[p, way], a_recv.at[p, way], peer(axis, k)))
        step_a.append(step)
    turn_centered(0, 2)
    step_b = []
    for p in range(PARTS):
        axis = ORDER[p][2]
        step = []
        for way, k in ((0, 1), (1, 3)):
            step_a[p][way].wait_recv()
            sel = only(full, axis, along(axis, k), 1)
            for part in range(2):
                value = here(p, only(sel, CUT[p], part * 2, 2))
                if part == way:
                    value = value + a_recv[p, way].astype(jnp.float32)
                value = value.astype(jnp.bfloat16)
                b_send[p, way, part] = value
            step.append(remote(b_send.at[p, way], b_recv.at[p, way], peer(axis, k)))
        step_b.append(step)
    turn_centered(2, 4)
    step_c = []
    for p in range(PARTS):
        axis = ORDER[p][2]
        sel = only(full, axis, pos[axis], 1)
        for way in range(2):
            step_b[p][way].wait_recv()
        for part in range(2):
            value = here(p, only(sel, CUT[p], part * 2, 2))
            value = value + b_recv[p, 0, part].astype(jnp.float32) + b_recv[p, 1, part].astype(jnp.float32)
            sum_two[p, part * 2 : part * 2 + 2] = value.reshape(2, 4, BLOCK, GROUP)
        axis = ORDER[p][1]
        step = []
        for j, k in enumerate((1, 3, 2)):
            i = along(axis, k)
            value = sum_two[p, :, i] if p == 1 else sum_two[p, i]
            c_send[p, j] = value.astype(jnp.bfloat16)
            step.append(remote(c_send.at[p, j], c_recv.at[p, j], peer(axis, k)))
        step_c.append(step)
    step_d = []
    kept = []
    for p in range(PARTS):
        axis = ORDER[p][1]
        value = sum_two[p, :, pos[axis]] if p == 1 else sum_two[p, pos[axis]]
        for j in range(3):
            step_c[p][j].wait_recv()
            value = value + c_recv[p, j].astype(jnp.float32)
        sum_two[p, 0] = value
        axis = ORDER[p][0]
        step = []
        for j, k in enumerate((1, 3, 2)):
            d_send[p, j] = sum_two[p, 0, along(axis, k)].astype(jnp.bfloat16)
            step.append(remote(d_send.at[p, j], d_recv.at[p, j], peer(axis, k)))
        step_d.append(step)
    for p in range(PARTS):
        value = sum_two[p, 0, pos[ORDER[p][0]]]
        for j in range(3):
            step_d[p][j].wait_recv()
            value = value + d_recv[p, j].astype(jnp.float32)
        kept.append((value - own_cen[p].astype(jnp.float32)).astype(jnp.bfloat16))

    put = []

    def last_turn():
        turn_centered(4, 6)
        put.append(local(cen_t, centered_t_out))

    gather(err, kept, nothing, nothing, last_turn)

    for t in range(ROWS // TILE):
        back = jnp.dot(wide(err, t), dec_t[...], preferred_element_type=jnp.float32)
        slope = jnp.where(
            codes[t].astype(jnp.float32) > 0.0, back * (2.0 / loss_norm) + norms[...], 0.0
        )
        slopes[t * TILE : (t + 1) * TILE, :] = slope.astype(jnp.bfloat16)
        put.append(
            local(slopes.at[pl.ds(t * TILE, TILE)], slopes_out.at[pl.ds(t * TILE, TILE)])
        )
    row = (m * 32 + lat) * 8
    holder = lax.div(row, 32)
    hx = lax.div(lax.rem(row, 32), BLOCK) * 2 + lax.rem(holder, 2)
    hyz = lax.div(holder, 2)
    hz = pl.ds(pl.multiple_of(lax.rem(hyz, 4) * BLOCK, BLOCK), BLOCK)
    upper = lax.rem(row, BLOCK) > 0
    for g in range(2 * PARTS):
        rows = err[g, hx, lax.div(hyz, 4), hz, :].astype(jnp.float32)
        error_out[:, g * GROUP : (g + 1) * GROUP] = jnp.where(upper, rows[8:], rows[:8])
    for copy in put:
        copy.wait()
    for copy in sent:
        copy.wait_send()


N_REMOTE = 3 + 2 * PARTS * (3 + 3 + 2 + 2 + 5) + 4 + PARTS * (2 + 2 + 3 + 3)
N_LOCAL = 4 + 2 + 1 + 1 + 4


def exchange(resid, terms, dec_bias, enc_weight, enc_bias, dec_weight):
    bf16, f32 = jnp.bfloat16, jnp.float32
    anywhere = pl.BlockSpec(memory_space=pl.ANY)
    return pl.pallas_call(
        exchange_kernel,
        out_shape=(
            jax.ShapeDtypeStruct((ROWS, LAT_DEV), bf16),
            jax.ShapeDtypeStruct((D, ROWS), bf16),
            jax.ShapeDtypeStruct((8, D), f32),
        ),
        in_specs=[anywhere] * 6,
        out_specs=(anywhere, anywhere, pl.BlockSpec(memory_space=pltpu.VMEM)),
        scratch_shapes=[
            pltpu.VMEM((6, 4, 4, 64, GROUP), bf16),
            pltpu.VMEM((6, 4, 4, 64, GROUP), bf16),
            pltpu.VMEM((D, ROWS), bf16),
            pltpu.VMEM((D, LAT_DEV), bf16),
            pltpu.VMEM((2, LAT_DEV, HALF), bf16),
            pltpu.VMEM((D, LAT_DEV), bf16),
            pltpu.VMEM((1, LAT_DEV), f32),
            pltpu.VMEM((4, TILE, LAT_DEV), bf16),
            pltpu.VMEM((PARTS, 4, 4, 64, GROUP), bf16),
            pltpu.VMEM((PARTS, 4, 4, 64, GROUP), bf16),
            pltpu.VMEM((PARTS, 4, 4, 64, GROUP), f32),
            pltpu.VMEM((PARTS, 2, 128, GROUP), bf16),
            pltpu.VMEM((PARTS, 2, 128, GROUP), bf16),
            pltpu.VMEM((PARTS, 2, 2, 128, GROUP), bf16),
            pltpu.VMEM((PARTS, 2, 2, 128, GROUP), bf16),
            pltpu.VMEM((PARTS, 3, 4, BLOCK, GROUP), bf16),
            pltpu.VMEM((PARTS, 3, 4, BLOCK, GROUP), bf16),
            pltpu.VMEM((PARTS, 3, BLOCK, GROUP), bf16),
            pltpu.VMEM((PARTS, 3, BLOCK, GROUP), bf16),
            pltpu.VMEM((PARTS, 4, 4, BLOCK, GROUP), f32),
            pltpu.VMEM((ROWS, LAT_DEV), bf16),
            pltpu.VMEM((4, BLOCK, HALF), bf16),
            pltpu.VMEM((BLOCK, HALF), bf16),
            pltpu.VMEM((1, HALF), f32),
            pltpu.VMEM((1, LAT_DEV), f32),
            pltpu.VMEM((PARTS, BLOCK, GROUP), bf16),
            pltpu.SemaphoreType.DMA((N_REMOTE,)),
            pltpu.SemaphoreType.DMA((N_REMOTE,)),
            pltpu.SemaphoreType.DMA((N_LOCAL,)),
        ],
        compiler_params=pltpu.CompilerParams(
            collective_id=0, has_side_effects=True, vmem_limit_bytes=56 * 1024 * 1024
        ),
    )(resid, terms, dec_bias, enc_weight, enc_bias, dec_weight)


def adam_kernel(cen_t, slopes, weight, first, second, error, weight_new, first_new, second_new, error_new):
    corr_one = 1.0 - beta_one**STEP
    corr_two = 1.0 - beta_two**STEP
    grad = jnp.dot(cen_t[...], slopes[...], preferred_element_type=jnp.float32)
    one = beta_one * first[...] + (1.0 - beta_one) * grad
    two = beta_two * second[...] + (1.0 - beta_two) * grad * grad
    first_new[...] = one
    second_new[...] = two
    change = one / corr_one / (jnp.sqrt(two / corr_two) + adam_eps)
    weight_new[...] = (weight[...].astype(jnp.float32) - learn_rate * change).astype(jnp.bfloat16)

    @pl.when(pl.program_id(0) == 0)
    def _():
        error_new[...] = error[...].astype(jnp.bfloat16)


def adam(cen_t, slopes, weight, first, second, error):
    rows = 256
    tile = pl.BlockSpec((rows, LAT_DEV), lambda i: (i, 0))
    whole_error = pl.BlockSpec((8, D), lambda i: (0, 0))
    return pl.pallas_call(
        adam_kernel,
        grid=(D // rows,),
        out_shape=(
            jax.ShapeDtypeStruct((D, LAT_DEV), jnp.bfloat16),
            jax.ShapeDtypeStruct((D, LAT_DEV), jnp.float32),
            jax.ShapeDtypeStruct((D, LAT_DEV), jnp.float32),
            jax.ShapeDtypeStruct((8, D), jnp.bfloat16),
        ),
        in_specs=[
            pl.BlockSpec((rows, ROWS), lambda i: (i, 0)),
            pl.BlockSpec((ROWS, LAT_DEV), lambda i: (0, 0)),
            tile,
            tile,
            tile,
            whole_error,
        ],
        out_specs=(tile, tile, tile, whole_error),
        compiler_params=pltpu.CompilerParams(vmem_limit_bytes=32 * 1024 * 1024),
    )(cen_t, slopes, weight, first, second, error)


def on_device(
    resid_in, layer_terms, dec_bias, enc_weight, enc_bias, dec_weight, first_moment, second_moment
):
    slopes, cen_t, error = exchange(
        resid_in, layer_terms, dec_bias[None], enc_weight, enc_bias[None], dec_weight
    )
    return adam(cen_t, slopes, enc_weight, first_moment, second_moment, error)


def solution(mesh):
    in_specs = (
        P("lat", None),
        P("mp", "lat", None),
        P(),
        P(None, ("mp", "lat")),
        P(("mp", "lat")),
        P(("mp", "lat"), None),
        P(None, ("mp", "lat")),
        P(None, ("mp", "lat")),
    )
    out_specs = (
        P(None, ("mp", "lat")),
        P(None, ("mp", "lat")),
        P(None, ("mp", "lat")),
        P(("mp", "lat"), None),
    )
    return jax.shard_map(
        on_device, mesh=mesh, in_specs=in_specs, out_specs=out_specs, check_vma=False
    )
```

time: 1220 us -> 106 us (0.09)
  waiting for transfers between devices: 1160 us -> 0 us
  Pallas kernels: 0 us -> 94.3 us
  matrix products: 31.7 us -> 0 us
  between operations: 13.8 us -> 0.67 us
    reduce_scatter x1 -> x0, waiting for transfers between devices: 615 us -> none  [on_device(): lax.psum_scatter(jnp.dot(active, dec_weight, preferred_element_type=jnp.f...]
    all_gather x2 -> x0, waiting for transfers between devices: 510 us -> none  [the longest x1 364 us: on_device(): lax.all_gather(recon_error, ('mp', 'lat'), axis=0, tiled=True)]
    pallas_call x0 -> x2, Pallas kernels: none -> 94.3 us  [the longest x1 85.2 us: exchange(): pl.pallas_call(exchange_kernel, out_shape=(jax.ShapeDtypeStruct((ROWS, LA...]
    unnamed x5 -> x0, waiting for transfers between devices: 36.8 us -> none
    dot_general x3 -> x0, matrix products: 31.7 us -> none  [the longest x1 21 us: on_device(): lax.dot_general(piece, slopes, (((0,), (0,)), ((), ())), preferred_elemen...]
  transfers between devices with their start and end apart: 4 -> 0, of which waited for: 4 -> 0; matrix products, arithmetic and copies ran while one was open for 0% -> 0% of each run, Pallas kernels for 0% -> 0%
where the time goes in v1:
time: 106 us
  Pallas kernels  94.3 us (89%)
  local copies, waits for them, and re-layouts  10.6 us (10%)
    pallas_call x1, Pallas kernels, exchange(): pl.pallas_call(exchange_kernel, out_shape=(jax.ShapeDtypeStruct((ROWS, LA...  85.2 us
    unnamed x12, local copies, waits for them, and re-layouts  9.12 us
    pallas_call x1, Pallas kernels, adam(): pl.pallas_call(adam_kernel, grid=(D // rows,), out_shape=(jax.ShapeDtypeS...  9.1 us

profile of v1, /device:TPU:1, one launch (start us, length us, event | category | flops | bytes accessed | tf_op | source)
XLA Modules:
  0.0 105.6 jit_solution(10589867629736303365)
XLA Ops:
  0.6 0.0 copy-start
  0.6 1.5 %broadcast_in_dim.6.dec_bias = f32[1,2304]{1,0:T(1,128)} reshape(f32[2304]{0:T(1024)} %param.10) | data formatting | bytes 18432 | tf_op jit(solution)/shard_map/broadcast_in_dim | solution.py:445
  2.1 85.2 %shard_map.111 = (bf16[1024,512]{1,0:T(8,128)(2,1)}, bf16[2304,1024]{1,0:T(8,128)(2,1)}, f32[8,2304]{1,0:T(8,128)}) custom-call(bf16[32,2304]{1,0:T(8,128)(2,1)} %resid.1, bf16[1,32,2304]{2,1,0:T(8,128)(2,1)} %terms.1, f32[1,2304]{1,0:T(1,128)} %broadcast_in_dim.6.dec_bias, bf16[2304,512]{1,0:T(8,128)(2,1)} %weight.1, f32[1,512]{1,0:T(1,128)} %bitcast.1, ...), custom_call_target="tpu_custom_call" | custom-call | tf_op jit(solution)/shard_map/pallas_call | solution.py:353
  87.3 0.0 copy-done
  87.3 0.0 copy-start.1
  87.4 2.3 %copy-done.1 = f32[2304,512]{1,0:T(8,128)S(1)} copy-done((f32[2304,512]{1,0:T(8,128)S(1)}, f32[2304,512]{1,0:T(8,128)}, u32[]{:S(2)}) %copy-start.1) | copy-done | bytes 4718616
  89.7 0.0 copy-start.2
  89.7 2.3 %copy-done.2 = f32[2304,512]{1,0:T(8,128)S(1)} copy-done((f32[2304,512]{1,0:T(8,128)S(1)}, f32[2304,512]{1,0:T(8,128)}, u32[]{:S(2)}) %copy-start.2) | copy-done | bytes 4718616
  92.0 0.0 copy-start.3
  92.0 2.3 %copy-done.3 = bf16[2304,1024]{1,0:T(8,128)(2,1)S(1)} copy-done((bf16[2304,1024]{1,0:T(8,128)(2,1)S(1)}, bf16[2304,1024]{1,0:T(8,128)(2,1)}, u32[]{:S(2)}) %copy-start.3) | copy-done | bytes 4718616
  94.4 0.0 copy-start.4
  94.4 1.2 %copy-done.4 = bf16[1024,512]{1,0:T(8,128)(2,1)S(1)} copy-done((bf16[1024,512]{1,0:T(8,128)(2,1)S(1)}, bf16[1024,512]{1,0:T(8,128)(2,1)}, u32[]{:S(2)}) %copy-start.4) | copy-done | bytes 1048600
  95.6 0.0 copy-start.5
  95.6 0.9 copy-done.5
  96.5 9.1 %shard_map.112 = (bf16[2304,512]{1,0:T(8,128)(2,1)}, f32[2304,512]{1,0:T(8,128)}, f32[2304,512]{1,0:T(8,128)}, bf16[8,2304]{1,0:T(8,128)(2,1)}) custom-call(bf16[2304,1024]{1,0:T(8,128)(2,1)S(1)} %copy-done.3, bf16[1024,512]{1,0:T(8,128)(2,1)S(1)} %copy-done.4, bf16[2304,512]{1,0:T(8,128)(2,1)S(1)} %copy-done, f32[2304,512]{1,0:T(8,128)S(1)} %copy-done.1, ...), custom_call_target="tpu_custom_call" | custom-call | tf_op jit(solution)/shard_map/pallas_call | solution.py:419
Async XLA Ops:
  0.6 86.7 %copy-start = (bf16[2304,512]{1,0:T(8,128)(2,1)S(1)}, bf16[2304,512]{1,0:T(8,128)(2,1)}, u32[]{:S(2)}) copy-start(bf16[2304,512]{1,0:T(8,128)(2,1)} %weight.1) | copy-start | bytes 7077892
  87.3 2.3 %copy-start.1 = (f32[2304,512]{1,0:T(8,128)S(1)}, f32[2304,512]{1,0:T(8,128)}, u32[]{:S(2)}) copy-start(f32[2304,512]{1,0:T(8,128)} %first.1) | copy-start | bytes 14155780
  89.7 2.3 %copy-start.2 = (f32[2304,512]{1,0:T(8,128)S(1)}, f32[2304,512]{1,0:T(8,128)}, u32[]{:S(2)}) copy-start(f32[2304,512]{1,0:T(8,128)} %second.1) | copy-start | bytes 14155780
  92.0 2.3 %copy-start.3 = (bf16[2304,1024]{1,0:T(8,128)(2,1)S(1)}, bf16[2304,1024]{1,0:T(8,128)(2,1)}, u32[]{:S(2)}) copy-start(bf16[2304,1024]{1,0:T(8,128)(2,1)} %get-tuple-element.7.cen_t) | copy-start | bytes 14155780
  94.4 1.2 %copy-start.4 = (bf16[1024,512]{1,0:T(8,128)(2,1)S(1)}, bf16[1024,512]{1,0:T(8,128)(2,1)}, u32[]{:S(2)}) copy-start(bf16[1024,512]{1,0:T(8,128)(2,1)} %get-tuple-element.8.slopes) | copy-start | bytes 3145732
  95.6 0.9 copy-start.5
